TPU v7x, 512 devices: a whole 4x4x16 slice. The times are simulated.
512 devices in a mesh: cube: 8 (over x, core), front: 64 (over z, y).
Axes of the slice: x: 4, y: 4, z: 16, core: 2. Of those that a mesh axis runs over, the one named last changes fastest.
Arguments:
- leaf_blocks: float32 [8, 3840, 3840], P('cube', 'front'), may hold values from -8 to 11, as said below
- front_entries: float32 [7, 4096, 256], P(None, 'front'), may hold values from -0.001 to 3
- child_maps: int32 [7, 2, 60], replicated, may hold values from 0 to 63, as said below
Outputs:
- factor_columns: float32 [8, 3, 4096, 256], P('cube', None, 'front')
- top_block: float32 [3840, 3840], P('front')
Inputs may be any that keep to these rules, and one draw needn't show every extreme that they name: `child_maps`: for each node, each of the two rows lists distinct offsets, and the two rows together name every offset from 0 to 63. `leaf_blocks`: each leaf block is symmetric positive definite.
All inputs are finite; a program needn't handle non-finite values.
Results may differ from a plain program's by a relative error of at most 0.00033.
Values may be sent and summed in bfloat16 or wider, within the bound.
No kernel may reach another device: no remote copies, remote signals or barrier semaphores. Data moves between devices by JAX's collectives and lax.ppermute only.
A program may use at most 128 MiB of HBM per device.

v0:
```python
import jax
import jax.numpy as jnp
from jax import lax
from jax.sharding import PartitionSpec as P

PANEL = 256
HIGH = lax.Precision.HIGHEST


def swapped(value, axis, apart):
    mask = 2**apart
    pairs = [(source, source ^ mask) for source in range(lax.axis_size(axis))]
    return lax.ppermute(value, axis, pairs)


def onehot_table(mapping, width):
    return (mapping[:, None] == jnp.arange(width, dtype=jnp.int32)[None, :]).astype(jnp.float32)


def scatter_rows(block, mapping, devices, width):
    block_rows = block.shape[0]
    table = onehot_table(mapping, width)
    grid = block.reshape(block_rows, devices, block_rows)
    widened = jnp.einsum("ubv,vs->usb", grid, table, precision=HIGH)
    placed = jnp.einsum("usb,ut->tsb", widened, table, precision=HIGH)
    return placed.reshape(width, width * devices)


def cholesky_lower(pivot):
    symmetric = jnp.tril(pivot) + jnp.tril(pivot, -1).T
    return jnp.linalg.cholesky(symmetric)


def factor_front(matrix, devices, position, width, panel_rows):
    panel = panel_rows * devices
    trailing = width - panel_rows
    last_col = panel_rows * devices
    local_pivot = matrix[0:panel_rows, 0:last_col]
    gathered = lax.all_gather(local_pivot, "front", axis=0, tiled=True)
    pivot = jnp.transpose(gathered.reshape(devices, panel_rows, panel), (1, 0, 2)).reshape(
        panel, panel
    )
    factor = cholesky_lower(pivot)
    lhs_rows = matrix[panel_rows:, 0:last_col]
    solved = jax.scipy.linalg.solve_triangular(factor, lhs_rows.T, lower=True).T
    rounded = solved.astype(jnp.bfloat16)
    update = jnp.einsum(
        "ip,jp->ij",
        rounded,
        lax.all_gather(rounded, "front", axis=0, tiled=True),
        preferred_element_type=jnp.float32,
    )
    reordered = jnp.transpose(update.reshape(trailing, devices, trailing), (0, 2, 1)).reshape(
        trailing, trailing * devices
    )
    matrix = matrix.at[panel_rows:, last_col:].add(-reordered)
    upper = jnp.zeros((0, panel), jnp.float32)
    middle = lax.dynamic_index_in_dim(
        factor.reshape(panel_rows, devices, panel), position, 1, keepdims=False
    )
    columns = jnp.concatenate([upper, middle, solved], axis=0)
    return (columns, matrix)


def on_device(leaf_blocks, front_entries, child_maps):
    devices = lax.axis_size("front")
    position = lax.axis_index("front")
    subcube = lax.axis_index("cube")
    cube_count = lax.axis_size("cube")
    heights = cube_count.bit_length() - 1
    width = front_entries.shape[1]
    sep_rows = front_entries.shape[2] // devices
    panel_rows = PANEL // devices
    block_rows = leaf_blocks.shape[1]
    current = leaf_blocks[0]
    factors = []
    for height in range(heights):
        sibling = swapped(current, "cube", height)
        side_bit = jnp.right_shift(subcube, height) & 1
        left_block = jnp.where(side_bit == 0, current, sibling)
        right_block = jnp.where(side_bit == 0, sibling, current)
        node = jnp.right_shift(subcube + cube_count, height + 1)
        entries = lax.dynamic_index_in_dim(front_entries, node - 1, 0, keepdims=False)
        mappings = lax.dynamic_index_in_dim(child_maps, node - 1, 0, keepdims=False)
        placed_entries = jnp.transpose(
            entries.reshape(width, devices, sep_rows), (0, 2, 1)
        ).reshape(width, sep_rows * devices)
        zeros_rest = jnp.zeros((width, (width - sep_rows) * devices), jnp.float32)
        matrix = jnp.concatenate([placed_entries, zeros_rest], axis=1)
        matrix = matrix + scatter_rows(left_block, mappings[0], devices, width)
        matrix = matrix + scatter_rows(right_block, mappings[1], devices, width)
        factor_part, matrix = factor_front(matrix, devices, position, width, panel_rows)
        factors.append(factor_part)
        remain = matrix[sep_rows:, sep_rows * devices :].reshape(block_rows, block_rows, devices)
        current = jnp.transpose(remain, (0, 2, 1)).reshape(block_rows, devices * block_rows)
    return (jnp.stack(factors)[None], current)


def solution(mesh):
    in_specs = (P("cube", "front", None), P(None, "front", None), P())
    out_specs = (P("cube", None, "front", None), P("front", None))
    return jax.shard_map(
        on_device, mesh=mesh, in_specs=in_specs, out_specs=out_specs, check_vma=False
    )
```

profile of v0, /device:TPU:2, one launch (start us, length us, event | category | flops | bytes accessed | tf_op | source)
XLA Modules:
  0.0 1041.9 jit_solution(18427782496393358375)
XLA Ops:
  14.8 4.3 reshape.238
  40.7 88.9 %all-gather = f32[64,4,256]{2,1,0:T(4,128)S(1)} all-gather(f32[1,4,256]{2,1,0:T(4,128)S(1)} %slice_bitcast_fusion.17), channel_id=1, replica_groups=mesh['cube'=8,'front'=64] {'front'}, dimensions={0}, use_global_device_ids=true | all-gather | bytes 266240 | tf_op jit(solution)/shard_map/all_gather | solution.py:39
  130.1 11.7 %cholesky.172 = f32[128,128]{1,0:T(8,128)S(1)} custom-call(f32[128,128]{1,0:T(8,128)S(1)} %copy.109), custom_call_target="Cholesky" | custom-call | tf_op jit(solution)/shard_map/jit(cholesky)/cholesky | solution.py:31
  141.9 9.8 custom-call.15
  152.4 11.7 %cholesky.189 = f32[128,128]{1,0:T(8,128)S(1)} custom-call(f32[128,128]{1,0:T(8,128)S(1)} %copy.111), custom_call_target="Cholesky" | custom-call | tf_op jit(solution)/shard_map/jit(cholesky)/cholesky | solution.py:31
  170.1 19.7 %custom-call.16 = f32[2,128,128]{1,2,0:T(8,128)S(1)} custom-call(f32[2,128,128]{2,1,0:T(8,128)S(1)} %get-tuple-element.60), custom_call_target="InvertDiagBlocksLowerTriangular" | custom-call | tf_op jit(solution)/shard_map/jit(_solve_triangular)/triangular_solve | solution.py:45
  191.1 136.6 %all-gather.10.cloned.1.call-done = bf16[64,60,256]{2,1,0:T(8,128)(2,1)} async-done(((bf16[1,60,256]{2,1,0:T(8,128)(2,1)}), bf16[64,60,256]{2,1,0:T(8,128)(2,1)}) %all-gather.10.cloned.1.call-update) | async-done | bytes 1966096 | tf_op jit(solution)/shard_map/all_gather | solution.py:50
  350.6 13.7 %collective-permute-done.1 = f32[60,3840]{1,0:T(8,128)S(1)} collective-permute-done((f32[60,3840]{1,0:T(8,128)S(1)}, f32[60,3840]{1,0:T(8,128)S(1)}, u32[]{:S(2)}, u32[]{:S(2)}) %collective-permute-start.1) | collective-permute-done | bytes 921632 | tf_op jit(solution)/shard_map/ppermute | solution.py:13
  365.3 4.5 reshape.249
  391.1 80.7 %all-gather.2 = f32[64,4,256]{2,1,0:T(4,128)S(1)} all-gather(f32[1,4,256]{2,1,0:T(4,128)S(1)} %slice_bitcast_fusion.16), channel_id=1, replica_groups=mesh['cube'=8,'front'=64] {'front'}, dimensions={0}, use_global_device_ids=true | all-gather | bytes 266240 | tf_op jit(solution)/shard_map/all_gather | solution.py:39
  472.3 11.7 %cholesky.206 = f32[128,128]{1,0:T(8,128)S(1)} custom-call(f32[128,128]{1,0:T(8,128)S(1)} %copy.124), custom_call_target="Cholesky" | custom-call | tf_op jit(solution)/shard_map/jit(cholesky)/cholesky | solution.py:31
  484.7 9.8 custom-call.17
  495.2 11.7 %cholesky.223 = f32[128,128]{1,0:T(8,128)S(1)} custom-call(f32[128,128]{1,0:T(8,128)S(1)} %copy.126), custom_call_target="Cholesky" | custom-call | tf_op jit(solution)/shard_map/jit(cholesky)/cholesky | solution.py:31
  509.6 4.2 while.10
  513.8 19.7 %custom-call.18 = f32[2,128,128]{1,2,0:T(8,128)S(1)} custom-call(f32[2,128,128]{2,1,0:T(8,128)S(1)} %get-tuple-element.61), custom_call_target="InvertDiagBlocksLowerTriangular" | custom-call | tf_op jit(solution)/shard_map/jit(_solve_triangular)/triangular_solve | solution.py:45
  534.8 135.8 %all-gather.12.cloned.1.call-done = bf16[64,60,256]{2,1,0:T(8,128)(2,1)} async-done(((bf16[1,60,256]{2,1,0:T(8,128)(2,1)}), bf16[64,60,256]{2,1,0:T(8,128)(2,1)}) %all-gather.12.cloned.1.call-update) | async-done | bytes 1966096 | tf_op jit(solution)/shard_map/all_gather | solution.py:50
  695.9 12.8 %collective-permute-done.2 = f32[60,3840]{1,0:T(8,128)S(1)} collective-permute-done((f32[60,3840]{1,0:T(8,128)S(1)}, f32[60,3840]{1,0:T(8,128)S(1)}, u32[]{:S(2)}, u32[]{:S(2)}) %collective-permute-start.2) | collective-permute-done | bytes 921632 | tf_op jit(solution)/shard_map/ppermute | solution.py:13
  735.4 80.7 %all-gather.4 = f32[64,4,256]{2,1,0:T(4,128)S(1)} all-gather(f32[1,4,256]{2,1,0:T(4,128)S(1)} %slice_bitcast_fusion.15), channel_id=1, replica_groups=mesh['cube'=8,'front'=64] {'front'}, dimensions={0}, use_global_device_ids=true | all-gather | bytes 266240 | tf_op jit(solution)/shard_map/all_gather | solution.py:39
  816.6 11.7 %cholesky.240 = f32[128,128]{1,0:T(8,128)S(1)} custom-call(f32[128,128]{1,0:T(8,128)S(1)} %cholesky.276), custom_call_target="Cholesky" | custom-call | tf_op jit(solution)/shard_map/jit(cholesky)/cholesky | solution.py:31
  829.0 9.8 custom-call.19
  839.3 11.7 %cholesky.257 = f32[128,128]{1,0:T(8,128)S(1)} custom-call(f32[128,128]{1,0:T(8,128)S(1)} %convolution_subtract_fusion), custom_call_target="Cholesky" | custom-call | tf_op jit(solution)/shard_map/jit(cholesky)/cholesky | solution.py:31
  853.1 4.3 while.11
  857.3 19.7 %custom-call.20 = f32[2,128,128]{1,2,0:T(8,128)S(1)} custom-call(f32[2,128,128]{2,1,0:T(8,128)S(1)} %get-tuple-element.62), custom_call_target="InvertDiagBlocksLowerTriangular" | custom-call | tf_op jit(solution)/shard_map/jit(_solve_triangular)/triangular_solve | solution.py:45
  879.9 134.3 %all-gather.14.cloned.1.call-done = bf16[64,60,256]{2,1,0:T(8,128)(2,1)} async-done(((bf16[1,60,256]{2,1,0:T(8,128)(2,1)}), bf16[64,60,256]{2,1,0:T(8,128)(2,1)}) %all-gather.14.cloned.1.call-update) | async-done | bytes 1966096 | tf_op jit(solution)/shard_map/all_gather | solution.py:50
  (198 shorter events, 175.0 us)
Async XLA Ops:
  7.2 6.5 copy-start
  7.2 320.5 %all-gather.10.cloned.1.call-start = ((), (), s32[]{:S(2)}) async-start(), calls=%async_computation | async-start | bytes 2129920 | tf_op jit(solution)/shard_map/all_gather | solution.py:50
  8.5 5.2 collective-permute-start
  129.8 36.2 %copy-start.3 = (s32[2]{0:T(128)S(1)}, s32[2]{0:T(128)}, u32[]{:S(2)}) copy-start(s32[2]{0:T(128)} %iota_multiply_fusion) | copy-start | bytes 28
  191.1 479.6 %all-gather.12.cloned.1.call-start = ((), (), s32[]{:S(2)}) async-start(), calls=%async_computation.1 | async-start | bytes 2129920 | tf_op jit(solution)/shard_map/all_gather | solution.py:50
  347.8 16.5 %collective-permute-start.1 = (f32[60,3840]{1,0:T(8,128)S(1)}, f32[60,3840]{1,0:T(8,128)S(1)}, u32[]{:S(2)}, u32[]{:S(2)}) collective-permute-start(f32[60,3840]{1,0:T(8,128)S(1)} %reshape.248), channel_id=1, source_target_pairs={{0,128},{64,192},{128,0},{192,64},{256,384},{320,448},{384,256},{4... | collective-permute-start | bytes 2764808 | tf_op jit(solution)/shard_map/ppermute | solution.py:13
  534.8 479.4 %all-gather.14.cloned.1.call-start = ((), (), s32[]{:S(2)}) async-start(), calls=%async_computation.2 | async-start | bytes 2129920 | tf_op jit(solution)/shard_map/all_gather | solution.py:50
  687.9 7.7 copy-start.1
  690.7 18.0 %collective-permute-start.2 = (f32[60,3840]{1,0:T(8,128)S(1)}, f32[60,3840]{1,0:T(8,128)S(1)}, u32[]{:S(2)}, u32[]{:S(2)}) collective-permute-start(f32[60,3840]{1,0:T(8,128)S(1)} %reshape.259), channel_id=1, source_target_pairs={{0,256},{64,320},{128,384},{192,448},{256,0},{320,64},{384,128},{4... | collective-permute-start | bytes 2764808 | tf_op jit(solution)/shard_map/ppermute | solution.py:13
  733.7 82.7 %copy-start.2 = (pred[256,256]{1,0:T(8,128)(4,1)S(1)}, pred[256,256]{1,0:T(8,128)(4,1)}, u32[]{:S(2)}) copy-start(pred[256,256]{1,0:T(8,128)(4,1)} %copy.136) | copy-start | bytes 196612
Sparse Core Ops, SparseCore 0:
  191.2 136.4 all-gather.9
  534.9 135.7 all-gather.11
  878.4 135.7 all-gather.13
where the time goes:
time: 1050 us; the launch traced here: 1040 us
  waiting for transfers between devices  433 us (41%)
  blocking collectives  250 us (24%)
  other arithmetic  178 us (17%)
  local copies, waits for them, and re-layouts  111 us (11%)
  matrix products  41.4 us (4%)
  between operations  18.8 us (2%)
    all_gather x3, waiting for transfers between devices, factor_front(): lax.all_gather(rounded, 'front', axis=0, tiled=True)  407 us
    all_gather x3, blocking collectives, factor_front(): gathered = lax.all_gather(local_pivot, 'front', axis=0, tiled=True)  250 us
    another operation x20, other arithmetic, cholesky_lower(): return jnp.linalg.cholesky(symmetric)  103 us
    another operation x7, other arithmetic, factor_front(): solved = jax.scipy.linalg.solve_triangular(factor, lhs_rows.T, lower=True).T  60.4 us
    ppermute x3, waiting for transfers between devices, swapped(): return lax.ppermute(value, axis, pairs)  26.5 us
    neg x9, local copies, waits for them, and re-layouts, factor_front(): matrix = matrix.at[panel_rows:, last_col:].add(-reordered)  24.2 us
    reshape x6, local copies, waits for them, and re-layouts, scatter_rows(): grid = block.reshape(block_rows, devices, block_rows)  21.7 us
  transfers between devices with their start and end apart: 6, of which 5 were waited for; matrix products, arithmetic and copies ran while one was open for 1% of the time, Pallas kernels for 0%

commit v1 on v0

--- a/solution.py
+++ b/solution.py
@@ -5,6 +5,11 @@
 
 PANEL = 256
 HIGH = lax.Precision.HIGHEST
+
+
+def all_by_exchange(block, mesh_axis, along):
+    sent = jnp.stack([block] * lax.axis_size(mesh_axis))
+    return jnp.concatenate(lax.all_to_all(sent, mesh_axis, 0, 0), axis=along)
 
 
 def swapped(value, axis, apart):
@@ -47,7 +52,7 @@
     update = jnp.einsum(
         "ip,jp->ij",
         rounded,
-        lax.all_gather(rounded, "front", axis=0, tiled=True),
+        all_by_exchange(rounded, "front", 0),
         preferred_element_type=jnp.float32,
     )
     reordered = jnp.transpose(update.reshape(trailing, devices, trailing), (0, 2, 1)).reshape(

time: 1050 us -> 844 us (0.80)
  the two profiles are of different devices: /device:TPU:2 before, /device:TPU:4 now
where the time goes in v1:
time: 844 us; the launch traced here: 840 us
  blocking collectives  414 us (49%)
  other arithmetic  181 us (21%)
  local copies, waits for them, and re-layouts  90.1 us (11%)
  waiting for transfers between devices  81.1 us (10%)
  matrix products  53.3 us (6%)
  starting transfers between devices  13.1 us (2%)
    all_gather x3, blocking collectives, factor_front(): gathered = lax.all_gather(local_pivot, 'front', axis=0, tiled=True)  254 us
    all_to_all x2, blocking collectives, all_by_exchange(): return jnp.concatenate(lax.all_to_all(sent, mesh_axis, 0, 0), axis=along)  161 us
    another operation x20, other arithmetic, cholesky_lower(): return jnp.linalg.cholesky(symmetric)  103 us
    another operation x7, other arithmetic, factor_front(): solved = jax.scipy.linalg.solve_triangular(factor, lhs_rows.T, lower=True).T  61.3 us
    all_to_all x1, waiting for transfers between devices, all_by_exchange(): return jnp.concatenate(lax.all_to_all(sent, mesh_axis, 0, 0), axis=along)  53.6 us
    ppermute x3, waiting for transfers between devices, swapped(): return lax.ppermute(value, axis, pairs)  27.5 us
    dot_general x6, matrix products, scatter_rows(): placed = jnp.einsum('usb,ut->tsb', widened, table, precision=HIGH)  24.9 us
    reshape x6, local copies, waits for them, and re-layouts, scatter_rows(): grid = block.reshape(block_rows, devices, block_rows)  21.8 us
  transfers between devices with their start and end apart: 4, of which 4 were waited for; matrix products, arithmetic and copies ran while one was open for 1% of the time, Pallas kernels for 0%

profile of v1, /device:TPU:4, one launch (start us, length us, event | category | flops | bytes accessed | tf_op | source)
XLA Modules:
  0.0 839.9 jit_solution(9639115073263175992)
XLA Ops:
  26.1 12.3 %fusion.8 = f32[64,64,64]{2,0,1:T(8,128)S(1)} fusion(f32[60,64,64]{2,1,0:T(8,128)S(1)} %convolution_bitcast_fusion.4, s32[60]{0:T(128)S(1)} %get-tuple-element.128), kind=kOutput, calls=%fused_computation.14 | convolution fusion | flops 188747520 | bytes 2031856 | tf_op jit(solution)/shard_map/usb,ut->tsb/dot_general | solution.py:30
  42.9 88.9 %all-gather = f32[64,4,256]{2,1,0:T(4,128)S(1)} all-gather(f32[1,4,256]{2,1,0:T(4,128)S(1)} %slice_bitcast_fusion.17), channel_id=1, replica_groups=mesh['cube'=8,'front'=64] {'front'}, dimensions={0}, use_global_device_ids=true | all-gather | bytes 266240 | tf_op jit(solution)/shard_map/all_gather | solution.py:44
  132.4 11.7 %cholesky.172 = f32[128,128]{1,0:T(8,128)S(1)} custom-call(f32[128,128]{1,0:T(8,128)S(1)} %copy.106), custom_call_target="Cholesky" | custom-call | tf_op jit(solution)/shard_map/jit(cholesky)/cholesky | solution.py:36
  144.1 9.8 %custom-call.15 = f32[1,128,128]{1,2,0:T(8,128)S(1)} custom-call(f32[1,128,128]{2,1,0:T(8,128)S(1)} %get-tuple-element.119), custom_call_target="InvertDiagBlocksLowerTriangular" | custom-call | tf_op jit(solution)/shard_map/jit(cholesky)/cholesky | solution.py:36
  154.6 11.7 %cholesky.189 = f32[128,128]{1,0:T(8,128)S(1)} custom-call(f32[128,128]{1,0:T(8,128)S(1)} %copy.108), custom_call_target="Cholesky" | custom-call | tf_op jit(solution)/shard_map/jit(cholesky)/cholesky | solution.py:36
  169.3 4.5 while.9
  173.8 19.7 %custom-call.16 = f32[2,128,128]{1,2,0:T(8,128)S(1)} custom-call(f32[2,128,128]{2,1,0:T(8,128)S(1)} %get-tuple-element.60), custom_call_target="InvertDiagBlocksLowerTriangular" | custom-call | tf_op jit(solution)/shard_map/jit(_solve_triangular)/triangular_solve | solution.py:50
  194.4 91.0 %all_to_all.15 = bf16[64,60,256]{2,1,0:T(8,128)(2,1)S(1)} all-to-all(bf16[64,60,256]{2,1,0:T(8,128)(2,1)S(1)} %stack.15), channel_id=1, replica_groups=mesh['cube'=8,'front'=64] {'front'}, dimensions={0} | all-to-all | bytes 3932160 | tf_op jit(solution)/shard_map/all_to_all | solution.py:12
  303.0 12.5 %collective-permute-done.1 = f32[60,3840]{1,0:T(8,128)S(1)} collective-permute-done((f32[60,3840]{1,0:T(8,128)S(1)}, f32[60,3840]{1,0:T(8,128)S(1)}, u32[]{:S(2)}, u32[]{:S(2)}) %collective-permute-start.1) | collective-permute-done | bytes 921632 | tf_op jit(solution)/shard_map/ppermute | solution.py:18
  342.7 81.3 %all-gather.1 = f32[64,4,256]{2,1,0:T(4,128)S(1)} all-gather(f32[1,4,256]{2,1,0:T(4,128)S(1)} %slice_bitcast_fusion.16), channel_id=1, replica_groups=mesh['cube'=8,'front'=64] {'front'}, dimensions={0}, use_global_device_ids=true | all-gather | bytes 266240 | tf_op jit(solution)/shard_map/all_gather | solution.py:44
  424.6 11.7 %cholesky.206 = f32[128,128]{1,0:T(8,128)S(1)} custom-call(f32[128,128]{1,0:T(8,128)S(1)} %copy.122), custom_call_target="Cholesky" | custom-call | tf_op jit(solution)/shard_map/jit(cholesky)/cholesky | solution.py:36
  437.0 9.8 %custom-call.17 = f32[1,128,128]{1,2,0:T(8,128)S(1)} custom-call(f32[1,128,128]{2,1,0:T(8,128)S(1)} %get-tuple-element.115), custom_call_target="InvertDiagBlocksLowerTriangular" | custom-call | tf_op jit(solution)/shard_map/jit(cholesky)/cholesky | solution.py:36
  447.5 11.7 %cholesky.223 = f32[128,128]{1,0:T(8,128)S(1)} custom-call(f32[128,128]{1,0:T(8,128)S(1)} %copy.124), custom_call_target="Cholesky" | custom-call | tf_op jit(solution)/shard_map/jit(cholesky)/cholesky | solution.py:36
  466.3 19.7 %custom-call.18 = f32[2,128,128]{1,2,0:T(8,128)S(1)} custom-call(f32[2,128,128]{2,1,0:T(8,128)S(1)} %get-tuple-element.61), custom_call_target="InvertDiagBlocksLowerTriangular" | custom-call | tf_op jit(solution)/shard_map/jit(_solve_triangular)/triangular_solve | solution.py:50
  486.9 69.7 %all_to_all.16 = bf16[64,60,256]{2,1,0:T(8,128)(2,1)S(1)} all-to-all(bf16[64,60,256]{2,1,0:T(8,128)(2,1)S(1)} %stack.17), channel_id=1, replica_groups=mesh['cube'=8,'front'=64] {'front'}, dimensions={0} | all-to-all | bytes 3932160 | tf_op jit(solution)/shard_map/all_to_all | solution.py:12
  573.7 14.5 %collective-permute-done.2 = f32[60,3840]{1,0:T(8,128)S(1)} collective-permute-done((f32[60,3840]{1,0:T(8,128)S(1)}, f32[60,3840]{1,0:T(8,128)S(1)}, u32[]{:S(2)}, u32[]{:S(2)}) %collective-permute-start.2) | collective-permute-done | bytes 921632 | tf_op jit(solution)/shard_map/ppermute | solution.py:18
  589.6 4.5 reshape.272
  615.4 83.2 %all-gather.2 = f32[64,4,256]{2,1,0:T(4,128)S(1)} all-gather(f32[1,4,256]{2,1,0:T(4,128)S(1)} %slice_bitcast_fusion.15), channel_id=1, replica_groups=mesh['cube'=8,'front'=64] {'front'}, dimensions={0}, use_global_device_ids=true | all-gather | bytes 266240 | tf_op jit(solution)/shard_map/all_gather | solution.py:44
  699.1 11.7 %cholesky.240 = f32[128,128]{1,0:T(8,128)S(1)} custom-call(f32[128,128]{1,0:T(8,128)S(1)} %cholesky.276), custom_call_target="Cholesky" | custom-call | tf_op jit(solution)/shard_map/jit(cholesky)/cholesky | solution.py:36
  711.4 9.8 %custom-call.19 = f32[1,128,128]{1,2,0:T(8,128)S(1)} custom-call(f32[1,128,128]{2,1,0:T(8,128)S(1)} %get-tuple-element.111), custom_call_target="InvertDiagBlocksLowerTriangular" | custom-call | tf_op jit(solution)/shard_map/jit(cholesky)/cholesky | solution.py:36
  721.8 11.7 %cholesky.257 = f32[128,128]{1,0:T(8,128)S(1)} custom-call(f32[128,128]{1,0:T(8,128)S(1)} %convolution_subtract_fusion), custom_call_target="Cholesky" | custom-call | tf_op jit(solution)/shard_map/jit(cholesky)/cholesky | solution.py:36
  740.6 19.7 %custom-call.20 = f32[2,128,128]{1,2,0:T(8,128)S(1)} custom-call(f32[2,128,128]{2,1,0:T(8,128)S(1)} %get-tuple-element.62), custom_call_target="InvertDiagBlocksLowerTriangular" | custom-call | tf_op jit(solution)/shard_map/jit(_solve_triangular)/triangular_solve | solution.py:50
  762.6 5.7 all-to-all-start.2
  771.3 53.6 %all-to-all-done.2 = bf16[64,60,256]{2,1,0:T(8,128)(2,1)S(1)} async-done(((bf16[64,60,256]{2,1,0:T(8,128)(2,1)}), bf16[64,60,256]{2,1,0:T(8,128)(2,1)S(1)}, u32[]{:S(2)}, u32[]{:S(2)}) %all-to-all-start.2) | async-done | bytes 1966112 | tf_op jit(solution)/shard_map/all_to_all | solution.py:12
  (188 shorter events, 165.8 us)
Async XLA Ops:
  0.6 5.8 copy-start.2
  2.0 4.5 collective-permute-start
  299.5 16.0 %collective-permute-start.1 = (f32[60,3840]{1,0:T(8,128)S(1)}, f32[60,3840]{1,0:T(8,128)S(1)}, u32[]{:S(2)}, u32[]{:S(2)}) collective-permute-start(f32[60,3840]{1,0:T(8,128)S(1)} %reshape.260), channel_id=1, source_target_pairs={{0,128},{64,192},{128,0},{192,64},{256,384},{320,448},{384,256},{4... | collective-permute-start | bytes 2764808 | tf_op jit(solution)/shard_map/ppermute | solution.py:18
  327.7 1.7 copy-start
  570.7 17.5 %collective-permute-start.2 = (f32[60,3840]{1,0:T(8,128)S(1)}, f32[60,3840]{1,0:T(8,128)S(1)}, u32[]{:S(2)}, u32[]{:S(2)}) collective-permute-start(f32[60,3840]{1,0:T(8,128)S(1)} %reshape.271), channel_id=1, source_target_pairs={{0,256},{64,320},{128,384},{192,448},{256,0},{320,64},{384,128},{4... | collective-permute-start | bytes 2764808 | tf_op jit(solution)/shard_map/ppermute | solution.py:18
  600.7 1.7 copy-start.1
  762.6 62.4 %all-to-all-start.2 = ((bf16[64,60,256]{2,1,0:T(8,128)(2,1)}), bf16[64,60,256]{2,1,0:T(8,128)(2,1)S(1)}, u32[]{:S(2)}, u32[]{:S(2)}) async-start(bf16[64,60,256]{2,1,0:T(8,128)(2,1)} %stack.20), calls=%async_computation.2 | async-start | bytes 4194304 | tf_op jit(solution)/shard_map/all_to_all | solution.py:12
